TPU v7x, 32 devices: a whole 2x2x4 slice. The times are simulated.
32 devices in a mesh: row: 8 (over z, core), col: 4 (over y, x).
Axes of the slice: x: 2, y: 2, z: 4, core: 2. Of those that a mesh axis runs over, the one named last changes fastest.
Arguments:
- genotypes: bfloat16 [5120, 16384], P(None, ('row', 'col')), may hold values from -5 to 5
- running: float32 [16384, 8, 4, 512], P('row', None, 'col'), as said below
- grid_map: int32 [8], replicated, may hold values from 0 to 7, each once
Outputs:
- factored: float32 [8, 8, 256, 8, 4, 512], P(None, 'row', None, None, 'col')
Inputs may be any that keep to these rules, and one draw needn't show every extreme that they name: running is symmetric, and in its first 128 rows each diagonal entry exceeds the sum of the magnitudes of the row's other entries among the first 128 columns. grid_map holds each of its values once.
All inputs are finite; a program needn't handle non-finite values.
Results may differ from a plain program's by a relative error of at most 0.0003.
Values may be sent and summed in bfloat16 or wider, within the bound.
A program may use at most 256 MiB of HBM per device.

v0:
```python
import jax
import jax.numpy as jnp
from jax import lax
from jax.sharding import PartitionSpec as P

NB = 128


def broadcast(array, axis, root):
    mine = lax.axis_index(axis) == root
    return lax.psum(jnp.where(mine, array, jnp.zeros_like(array)), axis)


def assemble(trail, row_factor, global_rows, col_index, col_width):
    col_pos = jnp.arange(col_width, dtype=jnp.int32)
    in_panel = jnp.logical_and(col_index == 0, col_pos < NB)
    padded = jnp.pad(row_factor, ((0, 0), (0, col_width - NB)))
    left_part = jnp.where(global_rows[:, None] >= col_pos[None, :], padded, jnp.zeros_like(padded))
    right_part = jnp.where(global_rows[:, None] < NB, jnp.zeros_like(trail), trail)
    return jnp.where(in_panel[None, :], left_part, right_part)


def on_device(genotypes, running, grid_map):
    rows_count = lax.axis_size("row")
    row_index = lax.axis_index("row")
    col_index = lax.axis_index("col")
    snp_count = genotypes.shape[0]
    shard_cols = running.shape[3]
    block_rows = running.shape[0]
    sub_rows = block_rows // rows_count
    col_width = running.shape[1] * shard_cols
    mine_rows = lax.all_gather(genotypes, "col", axis=1, tiled=True)
    product = lax.dot_general(
        mine_rows,
        lax.all_gather(genotypes, "row", axis=1, tiled=True),
        (((0,), (0,)), ((), ())),
        preferred_element_type=jnp.float32,
    )
    updated = running.reshape(block_rows, col_width) + product * (1.0 / snp_count)
    inverse_map = jnp.argsort(grid_map)
    leading = broadcast(updated[:NB, :NB], "row", 0)
    lower_factor = jnp.linalg.cholesky(leading)
    own_factor = lax.linalg.triangular_solve(
        lower_factor, updated[:, :NB], left_side=False, lower=True, transpose_a=True
    )
    factor_block = broadcast(own_factor, "col", 0)
    col_slice = lax.dynamic_slice_in_dim(factor_block, col_index * shard_cols, shard_cols, 0)
    col_factor = lax.all_gather(col_slice, "row", axis=0, tiled=True)
    trail = updated - jnp.dot(factor_block, col_factor.T, precision=lax.Precision.HIGHEST)
    global_rows = row_index * block_rows + jnp.arange(block_rows, dtype=jnp.int32)
    finished = assemble(trail, factor_block, global_rows, col_index, col_width)
    send_tiles = jnp.take(finished.reshape(rows_count, sub_rows, col_width), inverse_map, axis=0)
    result = lax.all_to_all(send_tiles, "row", split_axis=0, concat_axis=0, tiled=True)
    return result.reshape(rows_count, 1, sub_rows, rows_count, 1, shard_cols)


def solution(mesh):
    in_specs = (P(None, ("row", "col")), P("row", None, "col", None), P())
    out_specs = P(None, "row", None, None, "col", None)
    return jax.shard_map(
        on_device, mesh=mesh, in_specs=in_specs, out_specs=out_specs, check_vma=False
    )
```

profile of v0, /device:TPU:0, one launch (start us, length us, event | category | flops | bytes accessed | tf_op | source)
XLA Modules:
  0.0 1718.0 jit_solution(14046359197444044486)
XLA Ops:
  6.5 0.0 all-gather.4.cloned.1.call-start
  6.5 0.7 all-gather.4.cloned.1.call-update
  7.3 0.0 all-gather.6.cloned.1.call-start
  7.3 0.7 all-gather.6.cloned.1.call-update
  8.0 0.0 all-reduce.4.cloned.1.call-start
  8.1 99.3 %reduce.6 = f32[2048,8,512]{2,1,0:T(8,128)} reduce(f32[2048,8,1,512]{3,2,1,0:T(1,128)} %param.4, f32[]{:T(128)} %constant.82), dimensions={2}, to_apply=%param.4.reduce_sub_computation | reduce | bytes 67108864 | tf_op args[1]
  107.4 38.1 %copy.5 = f32[256,8,8,512]{3,1,2,0:T(8,128)} copy(f32[256,8,8,512]{3,2,1,0:T(8,128)} %bitcast.16) | data formatting | bytes 67108864
  145.5 59.5 %all-gather.4.cloned.1.call-done = bf16[5120,2048]{1,0:T(8,128)(2,1)} async-done(((bf16[5120,512]{1,0:T(8,128)(2,1)}), bf16[5120,2048]{1,0:T(8,128)(2,1)}) %all-gather.4.cloned.1.call-update) | async-done | bytes 20971536 | tf_op jit(solution)/shard_map/all_gather | solution.py:32
  205.0 360.5 %all-gather.6.cloned.1.call-done = bf16[5120,4096]{1,0:T(8,128)(2,1)} async-done(((bf16[5120,512]{1,0:T(8,128)(2,1)}), bf16[5120,4096]{1,0:T(8,128)(2,1)}) %all-gather.6.cloned.1.call-update) | async-done | bytes 41943056 | tf_op jit(solution)/shard_map/all_gather | solution.py:35
  565.5 0.0 copy-start
  565.5 101.1 %multiply_add_fusion = f32[2048,4096]{1,0:T(8,128)} fusion(f32[2048,4096]{1,0:T(8,128)} %bitcast.17, bf16[5120,2048]{1,0:T(8,128)(2,1)} %all-gather.4.cloned.1.call-done, bf16[5120,4096]{1,0:T(8,128)(2,1)} %all-gather.6.cloned.1.call-done), kind=kOutput, calls=%fused_computation.4 | convolution fusion | flops 85916123136 | bytes 130023424 | tf_op jit(solution)/shard_map/dot_general | solution.py:33
  666.7 1.5 slice_select_fusion
  668.1 0.0 all-reduce.4.cloned.1.call-update
  668.2 0.3 all-reduce.6.cloned.1.call-start
  668.4 52.1 %all-reduce.4.cloned.1.call-done = f32[128,128]{1,0:T(8,128)} async-done(((f32[128,128]{1,0:T(8,128)}), f32[128,128]{1,0:T(8,128)}) %all-reduce.4.cloned.1.call-update) | async-done | bytes 65552 | tf_op jit(solution)/shard_map/psum | solution.py:11
  720.5 0.9 copy.4
  721.4 0.9 fusion.3
  722.3 11.7 cholesky.15
  734.0 0.7 compare_reduce_fusion
  734.8 0.7 fusion.1
  735.5 9.8 custom-call.6
  745.3 3.2 convolution_select_fusion
  748.5 0.0 all-reduce.6.cloned.1.call-update
  748.5 0.3 all-gather.8.cloned.1.call-start
  748.8 51.4 %all-reduce.6.cloned.1.call-done = f32[2048,128]{1,0:T(8,128)} async-done(((f32[2048,128]{1,0:T(8,128)}), f32[2048,128]{1,0:T(8,128)}) %all-reduce.6.cloned.1.call-update) | async-done | bytes 1048592 | tf_op jit(solution)/shard_map/psum | solution.py:11
  800.2 1.7 constant_dynamic-slice_fusion
  801.9 0.0 all-gather.8.cloned.1.call-update
  801.9 0.0 copy-done
  802.0 1.0 sort.17
  803.0 28.2 %all-gather.8.cloned.1.call-done = f32[4096,128]{1,0:T(8,128)} async-done(((f32[512,128]{1,0:T(8,128)}), f32[4096,128]{1,0:T(8,128)}) %all-gather.8.cloned.1.call-update) | async-done | bytes 2097168 | tf_op jit(solution)/shard_map/all_gather | solution.py:48
  831.2 40.3 %select_select_fusion = f32[2048,4096]{1,0:T(8,128)} fusion(f32[2048,4096]{1,0:T(8,128)} %multiply_add_fusion, f32[2048,128]{1,0:T(8,128)} %all-reduce.6.cloned.1.call-done, s32[2048]{0:T(1024)S(1)} %iota_add_fusion, pred[2048]{0:T(1024)(128)(4,1)S(1)} %broadcast_compare_fusion, pred[4096]{0:T(1024)(128)(4,1)S(1)} %fusion.4, ...), kind=kOutput, calls=%fused_computation.3 | convolution fusion | flops 12926844928 | bytes 70268928 | tf_op jit(solution)/shard_map/dot_general | solution.py:49
  871.5 21.2 %fusion.5 = (f32[8,256,2048]{2,1,0:T(8,128)}, f32[8,256,2048]{2,1,0:T(8,128)}) fusion(f32[8,256,4096]{2,1,0:T(8,128)} %bitcast.18), kind=kLoop, calls=%fused_computation.26 | loop fusion | bytes 67108864 | tf_op jit(solution)/shard_map/jit(_take)/gather | solution.py:52
  892.6 13.7 gather_fusion
  906.4 14.2 gather_fusion.1
  920.6 12.9 maximum_select_fusion
  933.4 729.2 %all_to_all.5 = f32[8,256,4096]{2,1,0:T(8,128)} all-to-all(f32[8,256,4096]{2,1,0:T(8,128)S(1)} %maximum_select_fusion), channel_id=1, replica_groups=mesh['row'=8,'col'=4] {'row'}, dimensions={0} | all-to-all | bytes 67108864 | tf_op jit(solution)/shard_map/all_to_all | solution.py:53
  1662.7 48.3 %reshape.38 = f32[8,1,256,8,1,512]{5,4,3,2,1,0:T(1,128)} reshape(f32[8,256,4096]{2,1,0:T(8,128)} %all_to_all.5) | data formatting | bytes 67108864 | tf_op jit(solution)/shard_map/reshape | solution.py:54
  (8 shorter events, 0.1 us)
Async XLA Ops:
  6.5 198.5 %all-gather.4.cloned.1.call-start = ((), (), s32[]{:S(2)}) async-start(), calls=%async_computation.1 | async-start | bytes 26214400 | tf_op jit(solution)/shard_map/all_gather | solution.py:32
  7.3 558.3 %all-gather.6.cloned.1.call-start = ((), (), s32[]{:S(2)}) async-start(), calls=%async_computation.2 | async-start | bytes 47185920 | tf_op jit(solution)/shard_map/all_gather | solution.py:35
  8.0 712.5 %all-reduce.4.cloned.1.call-start = ((), (), s32[]{:S(2)}) async-start(), calls=%async_computation.3 | async-start | bytes 131072 | tf_op jit(solution)/shard_map/psum | solution.py:11
  565.5 236.4 %copy-start = (s32[8]{0:T(128)S(1)}, s32[8]{0:T(128)}, u32[]{:S(2)}) copy-start(s32[8]{0:T(128)} %param.5) | copy-start | bytes 100
  668.2 132.1 %all-reduce.6.cloned.1.call-start = ((), (), s32[]{:S(2)}) async-start(), calls=%async_computation.4 | async-start | bytes 2097152 | tf_op jit(solution)/shard_map/psum | solution.py:11
  748.5 82.7 %all-gather.8.cloned.1.call-start = ((), (), s32[]{:S(2)}) async-start(), calls=%async_computation.5 | async-start | bytes 2359296 | tf_op jit(solution)/shard_map/all_gather | solution.py:48
Sparse Core Ops, SparseCore 0:
  9.2 195.7 all-gather.3
  206.6 358.8 all-gather.5
  668.3 52.1 all-reduce.3
  748.6 51.5 all-reduce.5
  802.1 29.0 all-gather.7
where the time goes:
time: 1730 us; the launch traced here: 1720 us
  blocking collectives  729 us (42%)
  waiting for transfers between devices  553 us (32%)
  matrix products  145 us (8%)
  other arithmetic  139 us (8%)
  local copies, waits for them, and re-layouts  138 us (8%)
    all_to_all x1, blocking collectives, on_device(): lax.all_to_all(send_tiles, 'row', split_axis=0, concat_axis=0, tiled=True)  729 us
    all_gather x1, waiting for transfers between devices, on_device(): lax.all_gather(genotypes, 'row', axis=1, tiled=True)  361 us
    psum x2, waiting for transfers between devices, broadcast(): return lax.psum(jnp.where(mine, array, jnp.zeros_like(array)), axis)  103 us
    dot_general x1, matrix products, on_device(): lax.dot_general(mine_rows, lax.all_gather(genotypes, 'row', axis=1, tiled...  101 us
    unnamed x1, other arithmetic  99.3 us
    all_gather x1, waiting for transfers between devices, on_device(): mine_rows = lax.all_gather(genotypes, 'col', axis=1, tiled=True)  59.5 us
    gather x3, local copies, waits for them, and re-layouts, on_device(): jnp.take(finished.reshape(rows_count, sub_rows, col_width), inverse_map,...  49.1 us
    reshape x1, local copies, waits for them, and re-layouts, on_device(): return result.reshape(rows_count, 1, sub_rows, rows_count, 1, shard_cols)  48.3 us
  transfers between devices with their start and end apart: 5, of which 5 were waited for; matrix products, arithmetic and copies ran while one was open for 8% of the time, Pallas kernels for 0%

commit v1 on v0

v1 whole, which is shorter than its diff:
```python
import functools
import math

import jax
import jax.numpy as jnp
from jax import lax
from jax.experimental import pallas as pl
from jax.experimental.pallas import tpu as pltpu
from jax.sharding import PartitionSpec as P

NB = 128
LANES = 128
OCTAVES = 24
STEPS = 32766.0 / OCTAVES
TINY = 1.1754944e-38
HUGE = 3.4028235e38


def shift_perm(n, s):
    return [(i, (i + s) % n) for i in range(n)]


def gather_shifts(x, axis):
    n = lax.axis_size(axis)
    me = lax.axis_index(axis)
    parts = [x] + [lax.ppermute(x, axis, shift_perm(n, s)) for s in range(1, n)]
    order = lax.rem(me - jnp.arange(n, dtype=jnp.int32) + n, n)
    return jnp.take(jnp.stack(parts), order, axis=0)


def broadcast_first(x, axis):
    n = lax.axis_size(axis)
    me = lax.axis_index(axis)
    have = 1
    while have < n:
        count = min(have, n - have)
        got = lax.ppermute(x, axis, [(i, i + have) for i in range(count)])
        x = jnp.where(me < have, x, got)
        have += count
    return x


def split_bf16(x):
    hi = x.astype(jnp.bfloat16)
    lo = (x - hi.astype(jnp.float32)).astype(jnp.bfloat16)
    return hi, lo


def finish_kernel(where_ref, a_ref, b_ref, run_ref, fa_ref, fb_ref, fac_ref, code_ref, scale_ref,
                  *, first, parts, shard, sub, tile, inv_m, block_rows):
    i = pl.program_id(0)
    row0 = where_ref[0] * block_rows + i * tile
    first_col = where_ref[1] == 0
    chunks = shard // LANES
    grow = row0 + lax.broadcasted_iota(jnp.int32, (tile, LANES), 0)
    cpos = lax.broadcasted_iota(jnp.int32, (tile, LANES), 1)
    top = grow < NB
    run = run_ref.reshape(tile * parts * chunks, LANES)
    for p in range(parts):
        acc = jnp.dot(a_ref[...], b_ref[p], preferred_element_type=jnp.float32) * inv_m
        acc = acc - jnp.dot(fa_ref[...], fb_ref[p], preferred_element_type=jnp.float32)
        pieces = []
        for j in range(chunks):
            g0 = run[pl.ds(p * chunks + j, tile, stride=parts * chunks), :]
            v = acc[:, j * LANES:(j + 1) * LANES] + g0
            v = jnp.where(top, 0.0, v)
            if first and p == 0 and j == 0:
                panel = jnp.where(grow >= cpos, fac_ref[...], 0.0)
                v = jnp.where(first_col, panel, v)
            pieces.append(v)
        for t in range(tile // sub):
            rows = slice(t * sub, (t + 1) * sub)
            mags = [jnp.abs(v[rows]) for v in pieces]
            peak = functools.reduce(jnp.maximum, mags)
            peak = jnp.max(peak, axis=0, keepdims=True)
            peak = jnp.max(peak, axis=1, keepdims=True)
            top_log = jnp.log2(jnp.maximum(jnp.broadcast_to(peak, (8, LANES)), TINY))
            scale_ref[t, p:p + 1, :] = top_log[:1]
            off = (OCTAVES - top_log[:1]) * STEPS + 1.5
            for j in range(chunks):
                v = pieces[j][rows]
                code = jnp.log2(jnp.maximum(mags[j], TINY)) * STEPS + off
                code = jnp.where(mags[j] > 0.0, jnp.maximum(code, 0.0), 0.0)
                code = jnp.minimum(code, 32767.0).astype(jnp.int32)
                code = jnp.where(v < 0.0, -code, code)
                col = (p * chunks + j) * LANES
                code_ref[t * sub:(t + 1) * sub, col:col + LANES] = code.astype(jnp.int16)


def decode_kernel(at_ref, *refs, parts, shard, sub):
    code_ref, scale_ref = refs[:2]
    out_ref = refs[-1]
    chunks = shard // LANES
    out = out_ref.reshape(sub * parts * chunks, LANES)
    for p in range(parts):
        base = scale_ref[0, p:p + 1, :] - OCTAVES - 1.0 / STEPS
        for j in range(chunks):
            col = (p * chunks + j) * LANES
            code = code_ref[:, col:col + LANES].astype(jnp.int32)
            mag = jnp.abs(code).astype(jnp.float32)
            v = jnp.minimum(jnp.exp2(mag * (1.0 / STEPS) + base), HUGE)
            v = jnp.where(code == 0, 0.0, jnp.where(code < 0, -v, v))
            out[pl.ds(p * chunks + j, sub, stride=parts * chunks), :] = v


def on_device(genotypes, running, grid_map):
    rows_count = lax.axis_size("row")
    cols_count = lax.axis_size("col")
    row_index = lax.axis_index("row")
    col_index = lax.axis_index("col")
    snp_count, shard = genotypes.shape
    block_rows = running.shape[0]
    sub = block_rows // rows_count
    p_count = running.shape[1]
    chunks = shard // LANES
    lanes_count = p_count * chunks
    inv_m = 1.0 / snp_count
    halves = 2
    parts = p_count // halves
    tile = sub * max(1, 512 // sub)
    tile = math.gcd(tile, block_rows)

    cols = lax.all_gather(genotypes, "row", axis=0)

    lead = broadcast_first(broadcast_first(genotypes[:, :NB], "row"), "col")
    run_panel = broadcast_first(running[:, 0, 0, :NB], "col")
    run_lead = broadcast_first(run_panel[:NB], "row")
    dims = (((0,), (0,)), ((), ()))
    lead_block = run_lead + lax.dot_general(lead, lead, dims, preferred_element_type=jnp.float32) * inv_m
    own_panel = lax.dynamic_slice_in_dim(run_panel, col_index * shard, shard, 0)
    own_panel = own_panel + lax.dot_general(
        genotypes, lead, dims, preferred_element_type=jnp.float32) * inv_m
    lower = jnp.linalg.cholesky(lead_block)
    own_factor = lax.linalg.triangular_solve(
        lower, own_panel, left_side=False, lower=True, transpose_a=True)
    row_factor = gather_shifts(own_factor, "col").reshape(block_rows, NB)
    col_factor = gather_shifts(own_factor, "row")
    hi, lo = split_bf16(row_factor)
    fa = jnp.concatenate([hi, hi, lo], axis=1)
    hi, lo = split_bf16(jnp.swapaxes(col_factor, 1, 2))
    fb = jnp.concatenate([hi, lo, hi], axis=1)

    mine_rows = gather_shifts(genotypes.T, "col").reshape(block_rows, snp_count)

    run = running.reshape(block_rows, lanes_count, LANES)
    where = jnp.stack([row_index, col_index]).astype(jnp.int32)
    inverse_map = jnp.argsort(grid_map).astype(jnp.int32)
    width = parts * shard
    vmem = 60 * 1024 * 1024

    out = None
    for h in range(halves):
        codes, scales = pl.pallas_call(
            functools.partial(finish_kernel, first=h == 0, parts=parts, shard=shard, sub=sub,
                              tile=tile, inv_m=inv_m, block_rows=block_rows),
            grid_spec=pltpu.PrefetchScalarGridSpec(
                num_scalar_prefetch=1,
                grid=(block_rows // tile,),
                in_specs=[
                    pl.BlockSpec((tile, snp_count), lambda i, w: (i, 0)),
                    pl.BlockSpec((parts, snp_count, shard), lambda i, w, h=h: (h, 0, 0),
                                 pipeline_mode=pl.Buffered(1)),
                    pl.BlockSpec((tile, parts * chunks, LANES), lambda i, w, h=h: (i, h, 0)),
                    pl.BlockSpec((tile, 3 * NB), lambda i, w: (i, 0)),
                    pl.BlockSpec((parts, 3 * NB, shard), lambda i, w, h=h: (h, 0, 0)),
                    pl.BlockSpec((tile, NB), lambda i, w: (i, 0)),
                ],
                out_specs=[
                    pl.BlockSpec((tile, width), lambda i, w: (i, 0)),
                    pl.BlockSpec((tile // sub, parts, LANES), lambda i, w: (i, 0, 0)),
                ],
            ),
            out_shape=[
                jax.ShapeDtypeStruct((block_rows, width), jnp.int16),
                jax.ShapeDtypeStruct((rows_count, parts, LANES), jnp.float32),
            ],
            compiler_params=pltpu.CompilerParams(vmem_limit_bytes=vmem),
            cost_estimate=pl.CostEstimate(
                flops=2 * block_rows * snp_count * width,
                bytes_accessed=2 * snp_count * (block_rows + width) + 6 * block_rows * width,
                transcendentals=block_rows * width),
            name=f"finish_{h}",
        )(where, mine_rows, cols, run, fa, fb, row_factor)
        for s in range(rows_count):
            target = lax.rem(row_index + s, rows_count)
            k = lax.dynamic_index_in_dim(inverse_map, target, 0, keepdims=False)
            part = lax.dynamic_slice_in_dim(codes, k * sub, sub, 0)
            scale = lax.dynamic_slice_in_dim(scales, k, 1, 0)
            if s:
                part = lax.ppermute(part, "row", shift_perm(rows_count, s))
                scale = lax.ppermute(scale, "row", shift_perm(rows_count, s))
            source = lax.rem(row_index - s + rows_count, rows_count).reshape(1)
            args = [source, part, scale]
            specs = [
                pl.BlockSpec((sub, width), lambda i, at: (0, 0)),
                pl.BlockSpec((1, parts, LANES), lambda i, at: (0, 0, 0)),
            ]
            if out is not None:
                args.append(out)
                specs.append(pl.BlockSpec(memory_space=pl.ANY))
            out = pl.pallas_call(
                functools.partial(decode_kernel, parts=parts, shard=shard, sub=sub),
                grid_spec=pltpu.PrefetchScalarGridSpec(
                    num_scalar_prefetch=1,
                    grid=(1,),
                    in_specs=specs,
                    out_specs=pl.BlockSpec((None, sub, parts * chunks, LANES),
                                           lambda i, at, h=h: (at[0], 0, h, 0)),
                ),
                out_shape=jax.ShapeDtypeStruct((rows_count, sub, lanes_count, LANES), jnp.float32),
                input_output_aliases={3: 0} if out is not None else {},
                compiler_params=pltpu.CompilerParams(vmem_limit_bytes=vmem),
                cost_estimate=pl.CostEstimate(
                    flops=10 * sub * width, bytes_accessed=6 * sub * width,
                    transcendentals=sub * width),
                name="decode",
            )(*args)
    return out.reshape(rows_count, 1, sub, p_count, 1, shard)


def solution(mesh):
    in_specs = (P(None, ("row", "col")), P("row", None, "col", None), P())
    out_specs = P(None, "row", None, None, "col", None)
    return jax.shard_map(
        on_device, mesh=mesh, in_specs=in_specs, out_specs=out_specs, check_vma=False
    )
```

time: 1730 us -> 1210 us (0.70)
  blocking collectives: 729 us -> 0 us
  starting transfers between devices: 0.63 us -> 290 us
  Pallas kernels: 0 us -> 216 us
  matrix products: 145 us -> 5.74 us
  waiting for transfers between devices: 553 us -> 481 us
  local copies, waits for them, and re-layouts: 138 us -> 84.8 us
  other arithmetic: 139 us -> 91.8 us
  between operations: 13.7 us -> 34.6 us
    all_to_all x1 -> x0, blocking collectives: 729 us -> none  [on_device(): lax.all_to_all(send_tiles, 'row', split_axis=0, concat_axis=0, tiled=True)]
    ppermute x0 -> x51, waiting for transfers between devices: none -> 480 us  [the longest x10 279 us: broadcast_first(): got = lax.ppermute(x, axis, [(i, i + have) for i in range(count)])]
    all_gather x3 -> x1, waiting for transfers between devices: 448 us -> 0.01 us  [on_device(): cols = lax.all_gather(genotypes, 'row', axis=0)]
    ppermute x0 -> x51, starting transfers between devices: none -> 290 us  [the longest x14 110 us: on_device(): part = lax.ppermute(part, 'row', shift_perm(rows_count, s))]
    pallas_call x0 -> x18, Pallas kernels: none -> 216 us  [the longest x2 153 us: on_device(): pl.pallas_call(functools.partial(finish_kernel, first=h == 0, parts=parts...]
    dot_general x2, matrix products: 141 us -> 4.2 us  [the longest x1 3.37 us: on_device(): lax.dot_general(genotypes, lead, dims, preferred_element_type=jnp.float32)]
    psum x2 -> x0, waiting for transfers between devices: 103 us -> none  [broadcast(): return lax.psum(jnp.where(mine, array, jnp.zeros_like(array)), axis)]
    unnamed x1 -> x3, other arithmetic: 99.3 us -> 21 us
  transfers between devices with their start and end apart: 5 -> 52, of which waited for: 5 -> 24; matrix products, arithmetic and copies ran while one was open for 8% -> 14% of each run, Pallas kernels for 0% -> 5%
where the time goes in v1:
time: 1210 us; the launch traced here: 1200 us
  waiting for transfers between devices  481 us (40%)
  starting transfers between devices  290 us (24%)
  Pallas kernels  216 us (18%)
  other arithmetic  91.8 us (8%)
  local copies, waits for them, and re-layouts  84.8 us (7%)
  between operations  34.6 us (3%)
    ppermute x10, waiting for transfers between devices, broadcast_first(): got = lax.ppermute(x, axis, [(i, i + have) for i in range(count)])  279 us
    pallas_call x2, Pallas kernels, on_device(): pl.pallas_call(functools.partial(finish_kernel, first=h == 0, parts=parts...  153 us
    ppermute x14, starting transfers between devices, on_device(): part = lax.ppermute(part, 'row', shift_perm(rows_count, s))  110 us
    ppermute x13, starting transfers between devices, gather_shifts(): parts = [x] + [lax.ppermute(x, axis, shift_perm(n, s)) for s in range(1, n)]  107 us
    ppermute x14, waiting for transfers between devices, on_device(): part = lax.ppermute(part, 'row', shift_perm(rows_count, s))  105 us
    ppermute x14, waiting for transfers between devices, on_device(): scale = lax.ppermute(scale, 'row', shift_perm(rows_count, s))  76 us
    pallas_call x16, Pallas kernels, on_device(): pl.pallas_call(functools.partial(decode_kernel, parts=parts, shard=shard,...  62.3 us
    ppermute x14, starting transfers between devices, on_device(): scale = lax.ppermute(scale, 'row', shift_perm(rows_count, s))  39.3 us
  transfers between devices with their start and end apart: 52, of which 24 were waited for; matrix products, arithmetic and copies ran while one was open for 14% of the time, Pallas kernels for 5%

profile of v1, /device:TPU:0, one launch (start us, length us, event | category | flops | bytes accessed | tf_op | source)
XLA Modules:
  0.0 1203.9 jit_solution(17481739017750011398)
XLA Ops:
  7.3 2.5 slice.20
  9.7 3.5 collective-permute-start.5
  13.2 3.3 collective-permute-start.2
  19.7 4.4 collective-permute-start.3
  25.8 4.2 collective-permute-start.6
  36.9 225.5 %collective-permute-done.3 = f32[2048,128]{0,1:T(8,128)S(1)} collective-permute-done((f32[2048,128]{0,1:T(8,128)S(1)}, f32[2048,128]{0,1:T(8,128)S(1)}, u32[]{:S(2)}, u32[]{:S(2)}) %collective-permute-start.3) | collective-permute-done | bytes 1048608 | tf_op jit(solution)/shard_map/ppermute | solution.py:37
  264.3 6.3 collective-permute-start.7
  270.6 13.7 %collective-permute-done.4 = f32[2048,128]{0,1:T(8,128)S(1)} collective-permute-done((f32[2048,128]{0,1:T(8,128)S(1)}, f32[2048,128]{0,1:T(8,128)S(1)}, u32[]{:S(2)}, u32[]{:S(2)}) %collective-permute-start.4) | collective-permute-done | bytes 1048608 | tf_op jit(solution)/shard_map/ppermute | solution.py:37
  286.7 4.0 collective-permute-start.11
  291.3 38.6 %collective-permute-done.11 = f32[128,128]{0,1:T(8,128)S(1)} collective-permute-done((f32[128,128]{0,1:T(8,128)S(1)}, f32[128,128]{0,1:T(8,128)S(1)}, u32[]{:S(2)}, u32[]{:S(2)}) %collective-permute-start.11) | collective-permute-done | bytes 65568 | tf_op jit(solution)/shard_map/ppermute | solution.py:37
  331.4 5.4 collective-permute-start.8
  336.9 15.3 %pad_maximum_fusion = bf16[4,512,5120]{1,2,0:T(8,128)(2,1)} fusion(bf16[1,512,5120]{1,2,0:T(8,128)(2,1)} %bitcast.7, bf16[1,512,5120]{1,2,0:T(8,128)(2,1)} %bitcast.6, bf16[1,512,5120]{1,2,0:T(8,128)(2,1)} %bitcast.5, bf16[1,512,5120]{1,2,0:T(8,128)(2,1)S(1)} %bitcast.86), kind=kLoop, calls=%fused_computation.5 | loop fusion | flops 31457280 | bytes 41943040 | tf_op jit(solution)/shard_map/stack | solution.py:28
  352.2 5.6 pad_maximum_fusion.2
  357.8 6.3 gather_fusion.4
  364.2 10.3 fusion.15
  374.5 7.0 gather_fusion.3
  381.5 7.0 gather_fusion.2
  390.2 21.0 %pad_maximum_fusion.1 = bf16[4,512,5120]{1,2,0:T(8,128)(2,1)} fusion(bf16[4,512,1536]{1,2,0:T(8,128)(2,1)} %gather_fusion.4, bf16[4,512,1792]{1,2,0:T(8,128)(2,1)} %gather_fusion.3, bf16[4,512,1792]{1,2,0:T(8,128)(2,1)} %gather_fusion.2), kind=kLoop, calls=%fused_computation.6 | loop fusion | flops 62914560 | bytes 41943040
  411.3 26.0 %copy.24 = bf16[4,512,5120]{2,1,0:T(8,128)(2,1)} copy(bf16[4,512,5120]{1,2,0:T(8,128)(2,1)} %pad_maximum_fusion.1) | data formatting | bytes 41943040
  438.2 11.7 cholesky.16
  451.2 9.8 custom-call.6
  461.1 3.4 fusion.1
  466.1 83.2 %collective-permute-start.17 = (f32[512,128]{1,0:T(8,128)S(1)}, f32[512,128]{1,0:T(8,128)S(1)}, u32[]{:S(2)}, u32[]{:S(2)}) collective-permute-start(f32[512,128]{1,0:T(8,128)S(1)} %get-tuple-element.61), channel_id=1, source_target_pairs={{0,8},{4,12},{8,16},{12,20},{16,24},{20,28},{24,0},{28,4},{1,9},{5... | collective-permute-start | bytes 786440 | tf_op jit(solution)/shard_map/ppermute | solution.py:26
  549.2 17.8 %bitcast_select_fusion.a_ref = bf16[2048,5120]{1,0:T(8,128)(2,1)} fusion(bf16[4,512,5120]{2,1,0:T(8,128)(2,1)} %copy.24, pred[2048]{0:T(1024)(128)(4,1)S(1)} %bitcast.97), kind=kLoop, calls=%fused_computation.7 | loop fusion | flops 10485760 | bytes 41945088 | tf_op jit(solution)/shard_map/jit(_take)/select_n | solution.py:28
  569.1 2.8 collective-permute-start.18
  572.6 17.1 %collective-permute-done.18 = f32[512,128]{1,0:T(8,128)S(1)} collective-permute-done((f32[512,128]{1,0:T(8,128)S(1)}, f32[512,128]{1,0:T(8,128)S(1)}, u32[]{:S(2)}, u32[]{:S(2)}) %collective-permute-start.18) | collective-permute-done | bytes 262176 | tf_op jit(solution)/shard_map/ppermute | solution.py:26
  589.9 11.2 collective-permute-start.21
  601.1 2.6 collective-permute-start.22
  610.3 3.7 gather_fusion.1
  620.9 76.6 %finish_1.1 = (s16[2048,2048]{1,0:T(8,128)(2,1)}, f32[8,4,128]{2,1,0:T(4,128)}) custom-call(s32[2]{0:T(128)} %pad_add_fusion.where_ref, bf16[2048,5120]{1,0:T(8,128)(2,1)} %bitcast_select_fusion.a_ref, bf16[8,5120,512]{2,1,0:T(8,128)(2,1)} %bitcast.99, f32[2048,32,128]{2,1,0:T(8,128)} %bitcast.95, bf16[2048,384]{1,0:T(8,128)(2,1)} %pad_maximum_fusion.4.fa_ref, ...), custom_call_target="tpu_custom_call" | custom-call | flops 42949672960 | bytes 67108864 | tf_op jit(solution)/shard_map/finish_1/pallas_call | solution.py:153
  697.5 76.8 %finish_0.1 = (s16[2048,2048]{1,0:T(8,128)(2,1)}, f32[8,4,128]{2,1,0:T(4,128)}) custom-call(s32[2]{0:T(128)} %pad_add_fusion.where_ref, bf16[2048,5120]{1,0:T(8,128)(2,1)} %bitcast_select_fusion.a_ref, bf16[8,5120,512]{2,1,0:T(8,128)(2,1)} %bitcast.100, f32[2048,32,128]{2,1,0:T(8,128)} %bitcast.96, bf16[2048,384]{1,0:T(8,128)(2,1)} %pad_maximum_fusion.4.fa_ref, ...), custom_call_target="tpu_custom_call" | custom-call | flops 42949672960 | bytes 67108864 | tf_op jit(solution)/shard_map/finish_0/pallas_call | solution.py:153
  774.2 7.8 constant_dynamic-slice_fusion.17
  783.1 3.3 constant_dynamic-slice_fusion.1
  786.4 3.7 collective-permute-start.37
  807.1 43.7 %collective-permute-done.28.refs_1_ = f32[1,4,128]{2,1,0:T(4,128)} collective-permute-done((f32[1,4,128]{2,1,0:T(4,128)S(1)}, f32[1,4,128]{2,1,0:T(4,128)}, u32[]{:S(2)}, u32[]{:S(2)}) %collective-permute-start.28) | collective-permute-done | bytes 2080 | tf_op jit(solution)/shard_map/ppermute | solution.py:191
  850.8 23.2 %collective-permute-start.30 = (f32[1,4,128]{2,1,0:T(4,128)S(1)}, f32[1,4,128]{2,1,0:T(4,128)}, u32[]{:S(2)}, u32[]{:S(2)}) collective-permute-start(f32[1,4,128]{2,1,0:T(4,128)S(1)} %get-tuple-element.48), channel_id=1, source_target_pairs={{0,16},{4,20},{8,24},{12,28},{16,0},{20,4},{24,8},{28,12},{1,17},{... | collective-permute-start | bytes 6152 | tf_op jit(solution)/shard_map/ppermute | solution.py:191
  875.6 4.0 collective-permute-done.32.refs_1_
  879.6 5.5 collective-permute-done.34.refs_1_
  891.2 3.6 collective-permute-done.40.refs_1_
  897.8 3.0 collective-permute-start.44
  906.3 3.0 collective-permute-start.48
  909.3 2.4 collective-permute-done.48.refs_1_
  911.9 4.6 collective-permute-done.50.refs_1_
  919.8 20.6 %collective-permute-done.41.refs_0_ = s16[256,2048]{1,0:T(8,128)(2,1)} collective-permute-done((s16[256,2048]{1,0:T(8,128)(2,1)}, s16[256,2048]{1,0:T(8,128)(2,1)}, u32[]{:S(2)}, u32[]{:S(2)}) %collective-permute-start.41) | collective-permute-done | bytes 1048608 | tf_op jit(solution)/shard_map/ppermute | solution.py:190
  940.4 102.2 %collective-permute-start.33 = (s16[256,2048]{1,0:T(8,128)(2,1)}, s16[256,2048]{1,0:T(8,128)(2,1)}, u32[]{:S(2)}, u32[]{:S(2)}) collective-permute-start(s16[256,2048]{1,0:T(8,128)(2,1)} %get-tuple-element.30), channel_id=1, source_target_pairs={{0,8},{4,12},{8,16},{12,20},{16,24},{20,28},{24,0},{28,4},{1,9},{5... | collective-permute-start | bytes 3145736 | tf_op jit(solution)/shard_map/ppermute | solution.py:190
  1042.6 43.7 %collective-permute-done.43.refs_0_ = s16[256,2048]{1,0:T(8,128)(2,1)} collective-permute-done((s16[256,2048]{1,0:T(8,128)(2,1)}, s16[256,2048]{1,0:T(8,128)(2,1)}, u32[]{:S(2)}, u32[]{:S(2)}) %collective-permute-start.43) | collective-permute-done | bytes 1048608 | tf_op jit(solution)/shard_map/ppermute | solution.py:190
  1086.3 41.0 %collective-permute-done.45.refs_0_ = s16[256,2048]{1,0:T(8,128)(2,1)} collective-permute-done((s16[256,2048]{1,0:T(8,128)(2,1)}, s16[256,2048]{1,0:T(8,128)(2,1)}, u32[]{:S(2)}, u32[]{:S(2)}) %collective-permute-start.45) | collective-permute-done | bytes 1048608 | tf_op jit(solution)/shard_map/ppermute | solution.py:190
  1127.7 3.9 decode.16.refs_2_
  1131.7 3.9 decode.17.refs_2_
  1135.6 3.9 decode.18.refs_2_
  1139.5 3.9 decode.19.refs_2_
  1143.3 3.9 decode.20.refs_2_
  1147.2 3.9 decode.21.refs_2_
  1151.1 3.9 decode.22.refs_2_
  1155.0 3.9 decode.23.refs_2_
  1158.8 3.9 decode.24.refs_2_
  1162.7 4.1 decode.25.refs_2_
  1166.8 4.0 collective-permute-start.26
  1170.8 3.9 decode.26.refs_2_
  1174.7 3.9 decode.27.refs_2_
  1178.6 3.9 decode.28.refs_2_
  1182.5 3.9 decode.29.refs_2_
  1188.2 3.9 decode.30.refs_2_
  1192.7 3.9 decode.31
  (172 shorter events, 61.2 us)
Async XLA Ops:
  6.5 614.3 %all-gather.3.cloned.1.call-start = ((), (), s32[]{:S(2)}) async-start(), calls=%async_computation | async-start | bytes 47185920 | tf_op jit(solution)/shard_map/all_gather | solution.py:123
  9.7 14.4 %collective-permute-start.5 = (bf16[5120,128]{1,0:T(8,128)(2,1)}, bf16[5120,128]{1,0:T(8,128)(2,1)}, u32[]{:S(2)}, u32[]{:S(2)}) collective-permute-start(bf16[5120,128]{1,0:T(8,128)(2,1)} %slice.20), channel_id=1, source_target_pairs={{0,4},{1,5},{2,6},{3,7}} | collective-permute-start | bytes 3932168 | tf_op jit(solution)/shard_map/ppermute | solution.py:37
  13.2 323.7 %collective-permute-start.2 = (bf16[512,5120]{0,1:T(8,128)(2,1)}, bf16[512,5120]{0,1:T(8,128)(2,1)}, u32[]{:S(2)}, u32[]{:S(2)}) collective-permute-start(bf16[512,5120]{0,1:T(8,128)(2,1)} %bitcast.81), channel_id=1, source_target_pairs={{0,3},{1,0},{2,1},{3,2},{4,7},{5,4},{6,5},{7,6},{8,11},{9,8},{10,9... | collective-permute-start | bytes 15728648 | tf_op jit(solution)/shard_map/ppermute | solution.py:26
  16.5 320.4 %collective-permute-start.1 = (bf16[512,5120]{0,1:T(8,128)(2,1)}, bf16[512,5120]{0,1:T(8,128)(2,1)}, u32[]{:S(2)}, u32[]{:S(2)}) collective-permute-start(bf16[512,5120]{0,1:T(8,128)(2,1)} %bitcast.82), channel_id=1, source_target_pairs={{0,2},{1,3},{2,0},{3,1},{4,6},{5,7},{6,4},{7,5},{8,10},{9,11},{10,... | collective-permute-start | bytes 15728648 | tf_op jit(solution)/shard_map/ppermute | solution.py:26
  17.0 319.9 %collective-permute-start = (bf16[512,5120]{0,1:T(8,128)(2,1)}, bf16[512,5120]{0,1:T(8,128)(2,1)}, u32[]{:S(2)}, u32[]{:S(2)}) collective-permute-start(bf16[512,5120]{0,1:T(8,128)(2,1)} %bitcast.83), channel_id=1, source_target_pairs={{0,1},{1,2},{2,3},{3,0},{4,5},{5,6},{6,7},{7,4},{8,9},{9,10},{10,1... | collective-permute-start | bytes 15728648 | tf_op jit(solution)/shard_map/ppermute | solution.py:26
  19.7 242.6 %collective-permute-start.3 = (f32[2048,128]{0,1:T(8,128)S(1)}, f32[2048,128]{0,1:T(8,128)S(1)}, u32[]{:S(2)}, u32[]{:S(2)}) collective-permute-start(f32[2048,128]{0,1:T(8,128)S(1)} %bitcast.90), channel_id=1, source_target_pairs={{0,1},{4,5},{8,9},{12,13},{16,17},{20,21},{24,25},{28,29}} | collective-permute-start | bytes 3145736 | tf_op jit(solution)/shard_map/ppermute | solution.py:37
  25.8 238.3 %collective-permute-start.6 = (bf16[5120,128]{1,0:T(8,128)(2,1)S(1)}, bf16[5120,128]{1,0:T(8,128)(2,1)}, u32[]{:S(2)}, u32[]{:S(2)}) collective-permute-start(bf16[5120,128]{1,0:T(8,128)(2,1)S(1)} %broadcast_select_fusion), channel_id=1, source_target_pairs={{0,8},{4,12},{1,9},{5,13},{2,10},{6,14},{3,11},{7,15}} | collective-permute-start | bytes 3932168 | tf_op jit(solution)/shard_map/ppermute | solution.py:37
  262.5 74.4 %slice-start = ((s8[5242880]{0:T(1024)(128)(4,1)}), s8[4194304]{0:T(1024)(128)(4,1)S(1)}, s32[]{:S(2)}) async-start(s8[5242880]{0:T(1024)(128)(4,1)} %bitcast.84), calls=%async_computation.1 | async-start | bytes 8388608
  262.5 21.9 %collective-permute-start.4 = (f32[2048,128]{0,1:T(8,128)S(1)}, f32[2048,128]{0,1:T(8,128)S(1)}, u32[]{:S(2)}, u32[]{:S(2)}) collective-permute-start(f32[2048,128]{0,1:T(8,128)S(1)} %broadcast_select_fusion.5), channel_id=1, source_target_pairs={{0,2},{1,3},{4,6},{5,7},{8,10},{9,11},{12,14},{13,15},{16,18},{17,... | collective-permute-start | bytes 3145736 | tf_op jit(solution)/shard_map/ppermute | solution.py:37
  264.3 67.0 %collective-permute-start.7 = (bf16[5120,128]{1,0:T(8,128)(2,1)S(1)}, bf16[5120,128]{1,0:T(8,128)(2,1)S(1)}, u32[]{:S(2)}, u32[]{:S(2)}) collective-permute-start(bf16[5120,128]{1,0:T(8,128)(2,1)S(1)} %broadcast_select_fusion.1), channel_id=1, source_target_pairs={{0,16},{4,20},{8,24},{12,28},{1,17},{5,21},{9,25},{13,29},{2,18},{... | collective-permute-start | bytes 3932168 | tf_op jit(solution)/shard_map/ppermute | solution.py:37
  284.5 2.2 collective-permute-start.10
  286.7 43.2 %collective-permute-start.11 = (f32[128,128]{0,1:T(8,128)S(1)}, f32[128,128]{0,1:T(8,128)S(1)}, u32[]{:S(2)}, u32[]{:S(2)}) collective-permute-start(f32[128,128]{0,1:T(8,128)S(1)} %broadcast_select_fusion.11), channel_id=1, source_target_pairs={{0,8},{4,12},{1,9},{5,13},{2,10},{6,14},{3,11},{7,15}} | collective-permute-start | bytes 196616 | tf_op jit(solution)/shard_map/ppermute | solution.py:37
  329.9 107.3 %collective-permute-start.12 = (f32[128,128]{0,1:T(8,128)S(1)}, f32[128,128]{0,1:T(8,128)S(1)}, u32[]{:S(2)}, u32[]{:S(2)}) collective-permute-start(f32[128,128]{0,1:T(8,128)S(1)} %broadcast_select_fusion.12), channel_id=1, source_target_pairs={{0,16},{4,20},{8,24},{12,28},{1,17},{5,21},{9,25},{13,29},{2,18},{... | collective-permute-start | bytes 196616 | tf_op jit(solution)/shard_map/ppermute | solution.py:37
  331.4 57.1 %collective-permute-start.8 = (bf16[5120,128]{1,0:T(8,128)(2,1)S(1)}, bf16[5120,128]{1,0:T(8,128)(2,1)}, u32[]{:S(2)}, u32[]{:S(2)}) collective-permute-start(bf16[5120,128]{1,0:T(8,128)(2,1)S(1)} %broadcast_select_fusion.2), channel_id=1, source_target_pairs={{0,1},{4,5},{8,9},{12,13},{16,17},{20,21},{24,25},{28,29}} | collective-permute-start | bytes 3932168 | tf_op jit(solution)/shard_map/ppermute | solution.py:37
  388.7 48.6 %collective-permute-start.9 = (bf16[5120,128]{1,0:T(8,128)(2,1)S(1)}, bf16[5120,128]{1,0:T(8,128)(2,1)S(1)}, u32[]{:S(2)}, u32[]{:S(2)}) collective-permute-start(bf16[5120,128]{1,0:T(8,128)(2,1)S(1)} %broadcast_select_fusion.3), channel_id=1, source_target_pairs={{0,2},{1,3},{4,6},{5,7},{8,10},{9,11},{12,14},{13,15},{16,18},{17,... | collective-permute-start | bytes 3932168 | tf_op jit(solution)/shard_map/ppermute | solution.py:37
  466.0 103.1 %collective-permute-start.16 = (f32[512,128]{1,0:T(8,128)S(1)}, f32[512,128]{1,0:T(8,128)S(1)}, u32[]{:S(2)}, u32[]{:S(2)}) collective-permute-start(f32[512,128]{1,0:T(8,128)S(1)} %get-tuple-element.61), channel_id=1, source_target_pairs={{0,4},{4,8},{8,12},{12,16},{16,20},{20,24},{24,28},{28,0},{1,5},{5... | collective-permute-start | bytes 786440 | tf_op jit(solution)/shard_map/ppermute | solution.py:26
  466.1 105.8 %collective-permute-start.17 = (f32[512,128]{1,0:T(8,128)S(1)}, f32[512,128]{1,0:T(8,128)S(1)}, u32[]{:S(2)}, u32[]{:S(2)}) collective-permute-start(f32[512,128]{1,0:T(8,128)S(1)} %get-tuple-element.61), channel_id=1, source_target_pairs={{0,8},{4,12},{8,16},{12,20},{16,24},{20,28},{24,0},{28,4},{1,9},{5... | collective-permute-start | bytes 786440 | tf_op jit(solution)/shard_map/ppermute | solution.py:26
  567.0 36.7 %collective-permute-start.15 = (f32[512,128]{1,0:T(8,128)S(1)}, f32[512,128]{1,0:T(8,128)S(1)}, u32[]{:S(2)}, u32[]{:S(2)}) collective-permute-start(f32[512,128]{1,0:T(8,128)S(1)} %get-tuple-element.61), channel_id=1, source_target_pairs={{0,3},{1,0},{2,1},{3,2},{4,7},{5,4},{6,5},{7,6},{8,11},{9,8},{10,9... | collective-permute-start | bytes 786440 | tf_op jit(solution)/shard_map/ppermute | solution.py:26
  567.0 36.7 %collective-permute-start.14 = (f32[512,128]{1,0:T(8,128)S(1)}, f32[512,128]{1,0:T(8,128)S(1)}, u32[]{:S(2)}, u32[]{:S(2)}) collective-permute-start(f32[512,128]{1,0:T(8,128)S(1)} %get-tuple-element.61), channel_id=1, source_target_pairs={{0,2},{1,3},{2,0},{3,1},{4,6},{5,7},{6,4},{7,5},{8,10},{9,11},{10,... | collective-permute-start | bytes 786440 | tf_op jit(solution)/shard_map/ppermute | solution.py:26
  568.2 35.6 %collective-permute-start.13 = (f32[512,128]{1,0:T(8,128)S(1)}, f32[512,128]{1,0:T(8,128)S(1)}, u32[]{:S(2)}, u32[]{:S(2)}) collective-permute-start(f32[512,128]{1,0:T(8,128)S(1)} %get-tuple-element.61), channel_id=1, source_target_pairs={{0,1},{1,2},{2,3},{3,0},{4,5},{5,6},{6,7},{7,4},{8,9},{9,10},{10,1... | collective-permute-start | bytes 786440 | tf_op jit(solution)/shard_map/ppermute | solution.py:26
  569.1 20.6 %collective-permute-start.18 = (f32[512,128]{1,0:T(8,128)S(1)}, f32[512,128]{1,0:T(8,128)S(1)}, u32[]{:S(2)}, u32[]{:S(2)}) collective-permute-start(f32[512,128]{1,0:T(8,128)S(1)} %get-tuple-element.61), channel_id=1, source_target_pairs={{0,12},{4,16},{8,20},{12,24},{16,28},{20,0},{24,4},{28,8},{1,13},{... | collective-permute-start | bytes 786440 | tf_op jit(solution)/shard_map/ppermute | solution.py:26
  571.9 18.0 %collective-permute-start.19 = (f32[512,128]{1,0:T(8,128)S(1)}, f32[512,128]{1,0:T(8,128)S(1)}, u32[]{:S(2)}, u32[]{:S(2)}) collective-permute-start(f32[512,128]{1,0:T(8,128)S(1)} %get-tuple-element.61), channel_id=1, source_target_pairs={{0,16},{4,20},{8,24},{12,28},{16,0},{20,4},{24,8},{28,12},{1,17},{... | collective-permute-start | bytes 786440 | tf_op jit(solution)/shard_map/ppermute | solution.py:26
  589.7 11.4 collective-permute-start.20
  589.9 16.8 %collective-permute-start.21 = (f32[512,128]{1,0:T(8,128)S(1)}, f32[512,128]{1,0:T(8,128)S(1)}, u32[]{:S(2)}, u32[]{:S(2)}) collective-permute-start(f32[512,128]{1,0:T(8,128)S(1)} %get-tuple-element.61), channel_id=1, source_target_pairs={{0,24},{4,28},{8,0},{12,4},{16,8},{20,12},{24,16},{28,20},{1,25},{... | collective-permute-start | bytes 786440 | tf_op jit(solution)/shard_map/ppermute | solution.py:26
  601.1 8.4 collective-permute-start.22
  782.1 134.4 %collective-permute-start.29 = (s16[256,2048]{1,0:T(8,128)(2,1)}, s16[256,2048]{1,0:T(8,128)(2,1)S(1)}, u32[]{:S(2)}, u32[]{:S(2)}) collective-permute-start(s16[256,2048]{1,0:T(8,128)(2,1)} %get-tuple-element.32), channel_id=1, source_target_pairs={{0,16},{4,20},{8,24},{12,28},{16,0},{20,4},{24,8},{28,12},{1,17},{... | collective-permute-start | bytes 3145736 | tf_op jit(solution)/shard_map/ppermute | solution.py:190
  782.1 134.5 %collective-permute-start.35 = (s16[256,2048]{1,0:T(8,128)(2,1)}, s16[256,2048]{1,0:T(8,128)(2,1)S(1)}, u32[]{:S(2)}, u32[]{:S(2)}) collective-permute-start(s16[256,2048]{1,0:T(8,128)(2,1)} %get-tuple-element.29), channel_id=1, source_target_pairs={{0,4},{4,8},{8,12},{12,16},{16,20},{20,24},{24,28},{28,0},{1,5},{5... | collective-permute-start | bytes 3145736 | tf_op jit(solution)/shard_map/ppermute | solution.py:190
  783.1 103.9 %copy-start.5 = (f32[8,4,128]{2,1,0:T(4,128)S(1)}, f32[8,4,128]{2,1,0:T(4,128)}, u32[]{:S(2)}) copy-start(f32[8,4,128]{2,1,0:T(4,128)} %get-tuple-element.14) | copy-start | bytes 49156
  786.4 131.9 %collective-permute-start.37 = (s16[256,2048]{1,0:T(8,128)(2,1)}, s16[256,2048]{1,0:T(8,128)(2,1)S(1)}, u32[]{:S(2)}, u32[]{:S(2)}) collective-permute-start(s16[256,2048]{1,0:T(8,128)(2,1)} %get-tuple-element.27), channel_id=1, source_target_pairs={{0,28},{4,0},{8,4},{12,8},{16,12},{20,16},{24,20},{28,24},{1,29},{... | collective-permute-start | bytes 3145736 | tf_op jit(solution)/shard_map/ppermute | solution.py:190
  790.1 129.3 %collective-permute-start.39 = (s16[256,2048]{1,0:T(8,128)(2,1)}, s16[256,2048]{1,0:T(8,128)(2,1)}, u32[]{:S(2)}, u32[]{:S(2)}) collective-permute-start(s16[256,2048]{1,0:T(8,128)(2,1)} %get-tuple-element.26), channel_id=1, source_target_pairs={{0,24},{4,28},{8,0},{12,4},{16,8},{20,12},{24,16},{28,20},{1,25},{... | collective-permute-start | bytes 3145736 | tf_op jit(solution)/shard_map/ppermute | solution.py:190
  805.9 44.9 %collective-permute-start.28 = (f32[1,4,128]{2,1,0:T(4,128)S(1)}, f32[1,4,128]{2,1,0:T(4,128)}, u32[]{:S(2)}, u32[]{:S(2)}) collective-permute-start(f32[1,4,128]{2,1,0:T(4,128)S(1)} %get-tuple-element.49), channel_id=1, source_target_pairs={{0,20},{4,24},{8,28},{12,0},{16,4},{20,8},{24,12},{28,16},{1,21},{... | collective-permute-start | bytes 6152 | tf_op jit(solution)/shard_map/ppermute | solution.py:191
  850.8 24.8 %collective-permute-start.30 = (f32[1,4,128]{2,1,0:T(4,128)S(1)}, f32[1,4,128]{2,1,0:T(4,128)}, u32[]{:S(2)}, u32[]{:S(2)}) collective-permute-start(f32[1,4,128]{2,1,0:T(4,128)S(1)} %get-tuple-element.48), channel_id=1, source_target_pairs={{0,16},{4,20},{8,24},{12,28},{16,0},{20,4},{24,8},{28,12},{1,17},{... | collective-permute-start | bytes 6152 | tf_op jit(solution)/shard_map/ppermute | solution.py:191
  875.6 4.0 collective-permute-start.32
  879.6 5.5 collective-permute-start.34
  885.1 4.8 collective-permute-start.36
  889.9 1.3 collective-permute-start.38
  891.2 240.4 %copy-start.8 = (f32[1,4,128]{2,1,0:T(4,128)}, f32[1,4,128]{2,1,0:T(4,128)S(1)}, u32[]{:S(2)}) copy-start(f32[1,4,128]{2,1,0:T(4,128)S(1)} %collective-permute-done.38.refs_1_) | copy-start | bytes 6148
  891.2 3.6 collective-permute-start.40
  894.8 236.8 %copy-start.9 = (f32[1,4,128]{2,1,0:T(4,128)}, f32[1,4,128]{2,1,0:T(4,128)S(1)}, u32[]{:S(2)}) copy-start(f32[1,4,128]{2,1,0:T(4,128)S(1)} %collective-permute-done.40.refs_1_) | copy-start | bytes 6148
  894.8 3.0 collective-permute-start.42
  897.8 233.8 %copy-start.10 = (f32[1,4,128]{2,1,0:T(4,128)}, f32[1,4,128]{2,1,0:T(4,128)S(1)}, u32[]{:S(2)}) copy-start(f32[1,4,128]{2,1,0:T(4,128)S(1)} %collective-permute-done.42.refs_1_) | copy-start | bytes 6148
  897.8 4.5 collective-permute-start.44
  902.4 229.2 %copy-start.11 = (f32[1,4,128]{2,1,0:T(4,128)}, f32[1,4,128]{2,1,0:T(4,128)S(1)}, u32[]{:S(2)}) copy-start(f32[1,4,128]{2,1,0:T(4,128)S(1)} %collective-permute-done.44.refs_1_) | copy-start | bytes 6148
  902.4 3.9 collective-permute-start.46
  906.3 225.3 %copy-start.12 = (f32[1,4,128]{2,1,0:T(4,128)}, f32[1,4,128]{2,1,0:T(4,128)S(1)}, u32[]{:S(2)}) copy-start(f32[1,4,128]{2,1,0:T(4,128)S(1)} %collective-permute-done.46.refs_1_) | copy-start | bytes 6148
  906.3 5.4 collective-permute-start.48
  911.7 220.0 %copy-start.13 = (f32[1,4,128]{2,1,0:T(4,128)}, f32[1,4,128]{2,1,0:T(4,128)S(1)}, u32[]{:S(2)}) copy-start(f32[1,4,128]{2,1,0:T(4,128)S(1)} %collective-permute-done.48.refs_1_) | copy-start | bytes 6148
  911.7 4.8 collective-permute-start.50
  916.5 215.2 %copy-start.14 = (f32[1,4,128]{2,1,0:T(4,128)}, f32[1,4,128]{2,1,0:T(4,128)S(1)}, u32[]{:S(2)}) copy-start(f32[1,4,128]{2,1,0:T(4,128)S(1)} %collective-permute-done.50.refs_1_) | copy-start | bytes 6148
  916.5 23.9 %collective-permute-start.41 = (s16[256,2048]{1,0:T(8,128)(2,1)}, s16[256,2048]{1,0:T(8,128)(2,1)}, u32[]{:S(2)}, u32[]{:S(2)}) collective-permute-start(s16[256,2048]{1,0:T(8,128)(2,1)} %get-tuple-element.25), channel_id=1, source_target_pairs={{0,20},{4,24},{8,28},{12,0},{16,4},{20,8},{24,12},{28,16},{1,21},{... | collective-permute-start | bytes 3145736 | tf_op jit(solution)/shard_map/ppermute | solution.py:190
  916.5 215.2 %copy-start.2 = (s16[256,2048]{1,0:T(8,128)(2,1)}, s16[256,2048]{1,0:T(8,128)(2,1)S(1)}, u32[]{:S(2)}) copy-start(s16[256,2048]{1,0:T(8,128)(2,1)S(1)} %collective-permute-done.29.refs_0_) | copy-start | bytes 3145732
  916.5 169.8 %collective-permute-start.43 = (s16[256,2048]{1,0:T(8,128)(2,1)}, s16[256,2048]{1,0:T(8,128)(2,1)}, u32[]{:S(2)}, u32[]{:S(2)}) collective-permute-start(s16[256,2048]{1,0:T(8,128)(2,1)} %get-tuple-element.24), channel_id=1, source_target_pairs={{0,16},{4,20},{8,24},{12,28},{16,0},{20,4},{24,8},{28,12},{1,17},{... | collective-permute-start | bytes 3145736 | tf_op jit(solution)/shard_map/ppermute | solution.py:190
  916.6 215.1 %copy-start.3 = (s16[256,2048]{1,0:T(8,128)(2,1)}, s16[256,2048]{1,0:T(8,128)(2,1)S(1)}, u32[]{:S(2)}) copy-start(s16[256,2048]{1,0:T(8,128)(2,1)S(1)} %collective-permute-done.35.refs_0_) | copy-start | bytes 3145732
  916.6 210.7 %collective-permute-start.45 = (s16[256,2048]{1,0:T(8,128)(2,1)}, s16[256,2048]{1,0:T(8,128)(2,1)}, u32[]{:S(2)}, u32[]{:S(2)}) collective-permute-start(s16[256,2048]{1,0:T(8,128)(2,1)} %get-tuple-element.23), channel_id=1, source_target_pairs={{0,12},{4,16},{8,20},{12,24},{16,28},{20,0},{24,4},{28,8},{1,13},{... | collective-permute-start | bytes 3145736 | tf_op jit(solution)/shard_map/ppermute | solution.py:190
  918.3 213.4 %copy-start.4 = (s16[256,2048]{1,0:T(8,128)(2,1)}, s16[256,2048]{1,0:T(8,128)(2,1)S(1)}, u32[]{:S(2)}) copy-start(s16[256,2048]{1,0:T(8,128)(2,1)S(1)} %collective-permute-done.37.refs_0_) | copy-start | bytes 3145732
  918.3 209.0 %collective-permute-start.47 = (s16[256,2048]{1,0:T(8,128)(2,1)}, s16[256,2048]{1,0:T(8,128)(2,1)}, u32[]{:S(2)}, u32[]{:S(2)}) collective-permute-start(s16[256,2048]{1,0:T(8,128)(2,1)} %get-tuple-element.22), channel_id=1, source_target_pairs={{0,8},{4,12},{8,16},{12,20},{16,24},{20,28},{24,0},{28,4},{1,9},{5... | collective-permute-start | bytes 3145736 | tf_op jit(solution)/shard_map/ppermute | solution.py:190
  919.4 207.8 %collective-permute-start.49 = (s16[256,2048]{1,0:T(8,128)(2,1)}, s16[256,2048]{1,0:T(8,128)(2,1)}, u32[]{:S(2)}, u32[]{:S(2)}) collective-permute-start(s16[256,2048]{1,0:T(8,128)(2,1)} %get-tuple-element.21), channel_id=1, source_target_pairs={{0,4},{4,8},{8,12},{12,16},{16,20},{20,24},{24,28},{28,0},{1,5},{5... | collective-permute-start | bytes 3145736 | tf_op jit(solution)/shard_map/ppermute | solution.py:190
  940.4 226.5 %collective-permute-start.33 = (s16[256,2048]{1,0:T(8,128)(2,1)}, s16[256,2048]{1,0:T(8,128)(2,1)}, u32[]{:S(2)}, u32[]{:S(2)}) collective-permute-start(s16[256,2048]{1,0:T(8,128)(2,1)} %get-tuple-element.30), channel_id=1, source_target_pairs={{0,8},{4,12},{8,16},{12,20},{16,24},{20,28},{24,0},{28,4},{1,9},{5... | collective-permute-start | bytes 3145736 | tf_op jit(solution)/shard_map/ppermute | solution.py:190
  1086.3 88.4 %collective-permute-start.31 = (s16[256,2048]{1,0:T(8,128)(2,1)}, s16[256,2048]{1,0:T(8,128)(2,1)}, u32[]{:S(2)}, u32[]{:S(2)}) collective-permute-start(s16[256,2048]{1,0:T(8,128)(2,1)} %get-tuple-element.31), channel_id=1, source_target_pairs={{0,12},{4,16},{8,20},{12,24},{16,28},{20,0},{24,4},{28,8},{1,13},{... | collective-permute-start | bytes 3145736 | tf_op jit(solution)/shard_map/ppermute | solution.py:190
  1127.3 55.2 %collective-permute-start.27 = (s16[256,2048]{1,0:T(8,128)(2,1)}, s16[256,2048]{1,0:T(8,128)(2,1)}, u32[]{:S(2)}, u32[]{:S(2)}) collective-permute-start(s16[256,2048]{1,0:T(8,128)(2,1)} %get-tuple-element.33), channel_id=1, source_target_pairs={{0,20},{4,24},{8,28},{12,0},{16,4},{20,8},{24,12},{28,16},{1,21},{... | collective-permute-start | bytes 3145736 | tf_op jit(solution)/shard_map/ppermute | solution.py:190
  1127.3 60.4 %collective-permute-start.25 = (s16[256,2048]{1,0:T(8,128)(2,1)}, s16[256,2048]{1,0:T(8,128)(2,1)}, u32[]{:S(2)}, u32[]{:S(2)}) collective-permute-start(s16[256,2048]{1,0:T(8,128)(2,1)} %get-tuple-element.34), channel_id=1, source_target_pairs={{0,24},{4,28},{8,0},{12,4},{16,8},{20,12},{24,16},{28,20},{1,25},{... | collective-permute-start | bytes 3145736 | tf_op jit(solution)/shard_map/ppermute | solution.py:190
  1127.3 64.8 %collective-permute-start.23 = (s16[256,2048]{1,0:T(8,128)(2,1)}, s16[256,2048]{1,0:T(8,128)(2,1)}, u32[]{:S(2)}, u32[]{:S(2)}) collective-permute-start(s16[256,2048]{1,0:T(8,128)(2,1)} %get-tuple-element.35), channel_id=1, source_target_pairs={{0,28},{4,0},{8,4},{12,8},{16,12},{20,16},{24,20},{28,24},{1,29},{... | collective-permute-start | bytes 3145736 | tf_op jit(solution)/shard_map/ppermute | solution.py:190
  1166.8 20.8 %collective-permute-start.26 = (f32[1,4,128]{2,1,0:T(4,128)S(1)}, f32[1,4,128]{2,1,0:T(4,128)S(1)}, u32[]{:S(2)}, u32[]{:S(2)}) collective-permute-start(f32[1,4,128]{2,1,0:T(4,128)S(1)} %copy-done.18), channel_id=1, source_target_pairs={{0,24},{4,28},{8,0},{12,4},{16,8},{20,12},{24,16},{28,20},{1,25},{... | collective-permute-start | bytes 6152 | tf_op jit(solution)/shard_map/ppermute | solution.py:191
  1174.7 17.4 %collective-permute-start.24 = (f32[1,4,128]{2,1,0:T(4,128)S(1)}, f32[1,4,128]{2,1,0:T(4,128)S(1)}, u32[]{:S(2)}, u32[]{:S(2)}) collective-permute-start(f32[1,4,128]{2,1,0:T(4,128)S(1)} %copy-done.17), channel_id=1, source_target_pairs={{0,28},{4,0},{8,4},{12,8},{16,12},{20,16},{24,20},{28,24},{1,29},{... | collective-permute-start | bytes 6152 | tf_op jit(solution)/shard_map/ppermute | solution.py:191
  (12 other events, 218.4 us)
Sparse Core Ops, SparseCore 0:
  9.0 414.5 all-gather.2
